TPU v7x, 32 devices: a whole 2x2x4 slice. The times are simulated.
32 devices in a mesh: dom: 8 (over z, core), head: 4 (over y, x).
Axes of the slice: x: 2, y: 2, z: 4, core: 2. Of those that a mesh axis runs over, the one named last changes fastest.
Arguments:
- features: bfloat16 [16384, 512], P(('dom', 'head')), may hold values from -16 to 16
- tile_pattern: int32 [128, 6, 128, 128], P(('dom', 'head')), may hold values 0 or 1
- tile_source: int32 [128, 6], P(('dom', 'head')), may hold values from 0 to 11
- serve_list: int32 [8, 4, 8, 1], P('dom', 'head'), may hold values from 0 to 3
- key_blocks: int32 [128, 2], P('dom'), may hold values from 0 to 15, all different within a row
- qkv_weight: bfloat16 [512, 1536], replicated, may hold values from -0.25 to 0.25
- attn_weight: bfloat16 [512, 512], replicated, may hold values from -0.25 to 0.25
- norm_gain: float32 [512], replicated, may hold values from 0.5 to 1.5
- expand_weight: bfloat16 [2048, 512], P('head'), may hold values from -0.25 to 0.25
- reduce_weight: bfloat16 [2048, 512], P('head'), may hold values from -0.125 to 0.125
Outputs:
- output: bfloat16 [16384, 512], P(('dom', 'head'))
Inputs may be any that keep to these rules, and one draw needn't show every extreme that they name: `key_blocks`: the 2 entries of a row are distinct.
All inputs are finite; a program needn't handle non-finite values. No bound on the sum of `tile_pattern` on one device may be relied on, other than what follows from the above.
Results may differ from a plain program's by a relative error of at most 0.01.
The roundings to bfloat16 on the way count: a program that leaves them out, or rounds other values in their place, can miss the bound.
Values may be sent and summed in bfloat16 or wider, within the bound.
A program may use at most 128 MiB of HBM per device.

v0:
```python
import math

import jax
import jax.numpy as jnp
from jax import lax
from jax.sharding import PartitionSpec as P

HEADS = 16
HDIM = 32


def shards(
    features,
    tile_pattern,
    tile_source,
    serve_list,
    key_blocks,
    qkv_weight,
    attn_weight,
    norm_gain,
    expand_weight,
    reduce_weight,
):
    blk_local = tile_pattern.shape[0]
    tile_count = tile_pattern.shape[1]
    block_rows = tile_pattern.shape[2]
    model_width = features.shape[1]
    head_devices = lax.axis_size("head")
    own_blocks = features.reshape(blk_local, block_rows, model_width)
    outgoing_ids = serve_list[0, 0].reshape(-1)
    outgoing = jnp.take(own_blocks, outgoing_ids, axis=0)
    incoming = lax.all_to_all(outgoing, "dom", split_axis=0, concat_axis=0, tiled=True)
    source_table = jnp.concatenate([own_blocks, incoming], axis=0)
    sources = jnp.take(source_table, tile_source.reshape(-1), axis=0)
    sources = sources.reshape(blk_local, tile_count, block_rows, model_width)
    summed = jnp.einsum(
        "btij,btjf->bif",
        tile_pattern.astype(jnp.bfloat16),
        sources,
        preferred_element_type=jnp.float32,
    )
    degree = jnp.sum(tile_pattern, axis=(1, 3)).astype(jnp.float32)
    aggregated = (
        (own_blocks.astype(jnp.float32) + summed) * lax.rsqrt(1.0 + degree)[:, :, None]
    ).astype(jnp.bfloat16)
    aggregated = aggregated.reshape(blk_local * block_rows, model_width)
    local_heads = HEADS // head_devices
    qkv_all = jnp.dot(aggregated, qkv_weight, preferred_element_type=jnp.float32).astype(
        jnp.bfloat16
    )
    qkv_heads = lax.all_to_all(qkv_all, "head", split_axis=1, concat_axis=0, tiled=True)
    rows_all = qkv_heads.shape[0]
    blk_part = rows_all // block_rows
    qkv_grid = qkv_heads.reshape(blk_part, block_rows, local_heads, 3, HDIM)
    queries = qkv_grid[:, :, :, 0, :]
    keys = qkv_grid[:, :, :, 1, :]
    values = qkv_grid[:, :, :, 2, :]
    group = math.gcd(blk_part, max(1, 512 // block_rows))
    turns = blk_part // group
    query_groups = queries.reshape(turns, group, block_rows, local_heads, HDIM)
    id_groups = key_blocks.reshape(turns, group * key_blocks.shape[1])
    score_scale = 1.0 / math.sqrt(HDIM)

    def attend(inputs):
        query_group, chosen_ids = inputs
        chosen_keys = jnp.take(keys, chosen_ids, axis=0).reshape(group, -1, local_heads, HDIM)
        chosen_values = jnp.take(values, chosen_ids, axis=0).reshape(group, -1, local_heads, HDIM)
        scores = (
            jnp.einsum(
                "gqhe,gkhe->ghqk", query_group, chosen_keys, preferred_element_type=jnp.float32
            )
            * score_scale
        )
        row_max = jnp.max(scores, axis=-1, keepdims=True)
        exp_terms = jnp.exp(scores - row_max)
        attn_weights = (exp_terms / jnp.sum(exp_terms, axis=-1, keepdims=True)).astype(jnp.bfloat16)
        context = jnp.einsum(
            "ghqk,gkhe->gqhe", attn_weights, chosen_values, preferred_element_type=jnp.float32
        )
        return context.astype(jnp.bfloat16)

    context = lax.map(attend, (query_groups, id_groups)).reshape(rows_all, local_heads * HDIM)
    node_context = lax.all_to_all(context, "head", split_axis=0, concat_axis=1, tiled=True)
    mixed = aggregated.astype(jnp.float32) + jnp.dot(
        node_context, attn_weight, preferred_element_type=jnp.float32
    )
    mean_square = jnp.mean(mixed * mixed, axis=-1, keepdims=True)
    normed = (mixed * lax.rsqrt(mean_square + 1e-06) * norm_gain).astype(jnp.bfloat16)
    expanded = lax.dot_general(
        normed,
        lax.all_gather(expand_weight, "head", axis=0, tiled=True),
        (((1,), (1,)), ((), ())),
        preferred_element_type=jnp.float32,
    )
    activated = jax.nn.gelu(expanded).astype(jnp.bfloat16)
    ffn_sum = jnp.dot(
        activated,
        lax.all_gather(reduce_weight, "head", axis=0, tiled=True),
        preferred_element_type=jnp.float32,
    )
    return (normed.astype(jnp.float32) + ffn_sum).astype(jnp.bfloat16)


def solution(mesh):
    placed = (
        P(("dom", "head"), None),
        P(("dom", "head"), None, None, None),
        P(("dom", "head"), None),
        P("dom", "head", None, None),
        P("dom", None),
        P(),
        P(),
        P(),
        P("head", None),
        P("head", None),
    )
    return jax.shard_map(
        shards, mesh=mesh, in_specs=placed, out_specs=P(("dom", "head"), None), check_vma=False
    )
```

profile of v0, /device:TPU:0, one launch (start us, length us, event | category | flops | bytes accessed | tf_op | source)
XLA Modules:
  0.0 192.1 jit_solution(2289170273175090484)
XLA Ops:
  6.5 0.8 fusion.59
  7.3 0.7 compare_and_fusion.1
  8.0 1.7 gather_fusion.2
  9.6 0.0 copy-start.7
  9.7 1.2 broadcast_select_fusion.2
  10.8 6.5 %all-to-all-start = ((bf16[8,128,512]{2,1,0:T(8,128)(2,1)}), bf16[8,128,512]{2,1,0:T(8,128)(2,1)}, u32[]{:S(2)}, u32[]{:S(2)}) async-start(bf16[8,128,512]{2,1,0:T(8,128)(2,1)} %broadcast_select_fusion.2), calls=%async_computation | async-start | bytes 2097152 | tf_op jit(solution)/shard_map/all_to_all | solution.py:32
  17.3 0.0 all-gather.3.cloned.1.call-start
  17.3 0.7 all-gather.3.cloned.1.call-update
  18.0 0.1 reshape.123
  18.1 0.2 reduce_sum.27
  18.3 25.7 %all-to-all-done = bf16[8,128,512]{2,1,0:T(8,128)(2,1)} async-done(((bf16[8,128,512]{2,1,0:T(8,128)(2,1)}), bf16[8,128,512]{2,1,0:T(8,128)(2,1)}, u32[]{:S(2)}, u32[]{:S(2)}) %all-to-all-start) | async-done | bytes 1048608 | tf_op jit(solution)/shard_map/all_to_all | solution.py:32
  44.0 1.5 pad_maximum_fusion
  45.5 2.5 %gather_fusion.3 = bf16[24,128,512]{2,1,0:T(8,128)(2,1)} fusion(bf16[12,128,512]{2,1,0:T(8,128)(2,1)S(1)} %pad_maximum_fusion, s32[1024]{0:T(1024)S(1)} %pad_clamp_fusion.1), kind=kCustom, calls=%fused_computation.3 | custom fusion | bytes 6291552 | tf_op jit(solution)/shard_map/jit(_take)/gather | solution.py:34
  48.0 3.4 %fusion.55 = bf16[4,128,512]{2,1,0:T(8,128)(2,1)S(1)} fusion(bf16[4,6,128,512]{3,2,1,0:T(8,128)(2,1)} %bitcast.79, pred[4,6]{1,0:T(4,128)(4,1)S(1)} %compare_and_fusion.2, bf16[4,128,512]{2,1,0:T(8,128)(2,1)} %bitcast.78, s32[4,6,128,128]{3,2,1,0:T(8,128)} %param.15, f32[4,128]{1,0:T(4,128)S(1)} %add_rsqrt_fusion.1), kind=kOutput, calls=%fused_computation.50 | convolution fusion | flops 405667840 | bytes 5769240 | tf_op jit(solution)/shard_map/btij,btjf->bif/dot_general | solution.py:36
  51.3 0.0 copy-start.5
  51.4 0.8 copy-done.5
  52.2 1.0 convolution_convert_fusion.1
  53.2 1.6 copy.42
  54.8 3.8 %all-to-all-start.1 = ((bf16[512,4,384]{0,2,1:T(8,128)(2,1)}), bf16[512,4,384]{0,2,1:T(8,128)(2,1)S(1)}, u32[]{:S(2)}, u32[]{:S(2)}) async-start(bf16[512,4,384]{0,2,1:T(8,128)(2,1)} %bitcast.75), calls=%async_computation.1 | async-start | bytes 3145728 | tf_op jit(solution)/shard_map/all_to_all | solution.py:51
  58.6 0.7 all-gather.5.cloned.1.call-update
  59.4 0.1 copy.31
  59.5 0.1 reshape.125
  59.5 23.9 %all-to-all-done.1 = bf16[512,4,384]{0,2,1:T(8,128)(2,1)S(1)} async-done(((bf16[512,4,384]{0,2,1:T(8,128)(2,1)}), bf16[512,4,384]{0,2,1:T(8,128)(2,1)S(1)}, u32[]{:S(2)}, u32[]{:S(2)}) %all-to-all-start.1) | async-done | bytes 1572896 | tf_op jit(solution)/shard_map/all_to_all | solution.py:51
  83.4 2.4 %copy.33 = bf16[4,512,384]{1,0,2:T(4,128)(2,1)} copy(bf16[4,512,384]{1,2,0:T(8,128)(2,1)S(1)} %bitcast.74) | data formatting | bytes 3145728 | tf_op jit(solution)/shard_map/all_to_all | solution.py:51
  85.8 2.6 %reshape.126 = bf16[16,128,4,3,32]{1,0,4,3,2:T(8,128)(2,1)S(1)} reshape(bf16[4,512,384]{1,0,2:T(4,128)(2,1)} %copy.33) | data formatting | bytes 3145728 | tf_op jit(solution)/shard_map/reshape | solution.py:54
  88.4 1.2 slice_bitcast_fusion
  89.6 3.5 %copy.35 = bf16[16,128,4,32]{3,2,1,0:T(4,128)(2,1)} copy(bf16[16,128,4,32]{1,0,3,2:T(8,128)(2,1)} %get-tuple-element.71) | data formatting | bytes 1048576 | tf_op jit(solution)/shard_map/while | solution.py:82
  93.2 2.1 %copy.36 = bf16[16,128,4,32]{3,2,1,0:T(4,128)(2,1)} copy(bf16[16,128,4,32]{1,0,3,2:T(8,128)(2,1)S(1)} %copy-done.2) | data formatting | bytes 1048576 | tf_op jit(solution)/shard_map/while | solution.py:82
  95.3 0.1 copy.34
  95.4 68.1 %while.10 = (s32[]{:T(128)}, bf16[4,4,128,4,32]{2,1,4,3,0:T(4,128)(2,1)}, s32[4,8]{1,0:T(4,128)S(1)}, bf16[16,128,4,32]{3,2,1,0:T(4,128)(2,1)}, bf16[4,4,128,4,3...) while((s32[]{:T(128)}, bf16[4,4,128,4,32]{2,1,4,3,0:T(4,128)(2,1)}, ...), condition=%wide.region_4.6_spmd, body=%wide.region_1.0_spmd.sunk | while | flops 70059312 | bytes 8409889 | solution.py:82
  95.5 3.0 %gather_fusion = bf16[8,128,4,32]{3,2,1,0:T(4,128)(2,1)S(1)} fusion(bf16[16,128,4,32]{3,2,1,0:T(4,128)(2,1)} %get-tuple-element.142, s32[1024]{0:T(1024)S(1)} %pad_clamp_fusion.4), kind=kCustom, calls=%fused_computation.1.clone.clone.1 | custom fusion | bytes 524320 | tf_op jit(solution)/shard_map/while/body/eval_jaxpr/jit(_take)/gather | solution.py:66
  98.5 4.0 %gather_fusion.1 = bf16[8,128,4,32]{3,2,1,0:T(4,128)(2,1)} fusion(bf16[16,128,4,32]{3,2,1,0:T(4,128)(2,1)} %get-tuple-element.140, s32[1024]{0:T(1024)S(1)} %pad_clamp_fusion.4), kind=kCustom, calls=%fused_computation.clone.clone.1 | custom fusion | bytes 524320 | tf_op jit(solution)/shard_map/while/body/eval_jaxpr/jit(_take)/gather | solution.py:67
  102.5 3.5 %broadcast_select_fusion.4 = (bf16[8,128,4,32]{3,2,1,0:T(4,128)(2,1)}, bf16[8,128,4,32]{3,2,1,0:T(4,128)(2,1)}) fusion(bf16[8,128,4,32]{3,2,1,0:T(4,128)(2,1)S(1)} %gather_fusion, pred[8]{0:T(512)(128)(4,1)S(1)} %get-tuple-element.118, bf16[8,128,4,32]{3,2,1,0:T(4,128)(2,1)} %gather_fusion.1), kind=kLoop, calls=%fused_computation.15.clone.1 | loop fusion | flops 262144 | bytes 1048584 | tf_op jit(solution)/shard_map/while/body/eval_jaxpr/jit(_take)/select_n | solution.py:66
  106.0 3.4 %fusion.86 = (f32[4,4,128]{2,1,0:T(4,128)S(1)}, f32[4,4,128,256]{3,2,1,0:T(8,128)}) fusion(bf16[4,256,4,32]{3,2,1,0:T(4,128)(2,1)} %bitcast.73, bf16[4,4,128,4,32]{2,4,3,1,0:T(8,128)(2,1)S(1)} %get-tuple-element.141, s32[]{:T(128)} %get-tuple-element.130), kind=kOutput, calls=%fused_computation.75.clone.1 | convolution fusion | flops 35127552 | bytes 2498564 | tf_op jit(solution)/shard_map/while/body/eval_jaxpr/sub | solution.py:75
  109.4 2.3 %fusion.87 = bf16[1,4,128,4,32]{2,4,3,1,0:T(8,128)(2,1)S(1)} fusion(bf16[4,256,4,32]{3,2,1,0:T(4,128)(2,1)S(1)} %bitcast.72, f32[4,4,128,256]{3,2,1,0:T(8,128)} %get-tuple-element.121, f32[4,4,128]{2,1,0:T(4,128)S(1)} %get-tuple-element.122), kind=kOutput, calls=%fused_computation.10.clone.1 | convolution fusion | flops 34668544 | bytes 2498560 | tf_op jit(solution)/shard_map/while/body/eval_jaxpr/ghqk,gkhe->gqhe/dot_general | solution.py:77
  111.7 0.8 copy_dynamic-update-slice_fusion.2
  112.5 3.0 %gather_fusion = bf16[8,128,4,32]{3,2,1,0:T(4,128)(2,1)S(1)} fusion(bf16[16,128,4,32]{3,2,1,0:T(4,128)(2,1)} %get-tuple-element.142, s32[1024]{0:T(1024)S(1)} %pad_clamp_fusion.4), kind=kCustom, calls=%fused_computation.1.clone.clone.1 | custom fusion | bytes 524320 | tf_op jit(solution)/shard_map/while/body/eval_jaxpr/jit(_take)/gather | solution.py:66
  115.5 4.0 %gather_fusion.1 = bf16[8,128,4,32]{3,2,1,0:T(4,128)(2,1)} fusion(bf16[16,128,4,32]{3,2,1,0:T(4,128)(2,1)} %get-tuple-element.140, s32[1024]{0:T(1024)S(1)} %pad_clamp_fusion.4), kind=kCustom, calls=%fused_computation.clone.clone.1 | custom fusion | bytes 524320 | tf_op jit(solution)/shard_map/while/body/eval_jaxpr/jit(_take)/gather | solution.py:67
  119.5 3.5 %broadcast_select_fusion.4 = (bf16[8,128,4,32]{3,2,1,0:T(4,128)(2,1)}, bf16[8,128,4,32]{3,2,1,0:T(4,128)(2,1)}) fusion(bf16[8,128,4,32]{3,2,1,0:T(4,128)(2,1)S(1)} %gather_fusion, pred[8]{0:T(512)(128)(4,1)S(1)} %get-tuple-element.118, bf16[8,128,4,32]{3,2,1,0:T(4,128)(2,1)} %gather_fusion.1), kind=kLoop, calls=%fused_computation.15.clone.1 | loop fusion | flops 262144 | bytes 1048584 | tf_op jit(solution)/shard_map/while/body/eval_jaxpr/jit(_take)/select_n | solution.py:66
  123.1 3.4 %fusion.86 = (f32[4,4,128]{2,1,0:T(4,128)S(1)}, f32[4,4,128,256]{3,2,1,0:T(8,128)}) fusion(bf16[4,256,4,32]{3,2,1,0:T(4,128)(2,1)} %bitcast.73, bf16[4,4,128,4,32]{2,4,3,1,0:T(8,128)(2,1)S(1)} %get-tuple-element.141, s32[]{:T(128)} %get-tuple-element.130), kind=kOutput, calls=%fused_computation.75.clone.1 | convolution fusion | flops 35127552 | bytes 2498564 | tf_op jit(solution)/shard_map/while/body/eval_jaxpr/sub | solution.py:75
  126.4 2.3 %fusion.87 = bf16[1,4,128,4,32]{2,4,3,1,0:T(8,128)(2,1)S(1)} fusion(bf16[4,256,4,32]{3,2,1,0:T(4,128)(2,1)S(1)} %bitcast.72, f32[4,4,128,256]{3,2,1,0:T(8,128)} %get-tuple-element.121, f32[4,4,128]{2,1,0:T(4,128)S(1)} %get-tuple-element.122), kind=kOutput, calls=%fused_computation.10.clone.1 | convolution fusion | flops 34668544 | bytes 2498560 | tf_op jit(solution)/shard_map/while/body/eval_jaxpr/ghqk,gkhe->gqhe/dot_general | solution.py:77
  128.7 0.8 copy_dynamic-update-slice_fusion.2
  129.5 3.0 %gather_fusion = bf16[8,128,4,32]{3,2,1,0:T(4,128)(2,1)S(1)} fusion(bf16[16,128,4,32]{3,2,1,0:T(4,128)(2,1)} %get-tuple-element.142, s32[1024]{0:T(1024)S(1)} %pad_clamp_fusion.4), kind=kCustom, calls=%fused_computation.1.clone.clone.1 | custom fusion | bytes 524320 | tf_op jit(solution)/shard_map/while/body/eval_jaxpr/jit(_take)/gather | solution.py:66
  132.6 4.0 %gather_fusion.1 = bf16[8,128,4,32]{3,2,1,0:T(4,128)(2,1)} fusion(bf16[16,128,4,32]{3,2,1,0:T(4,128)(2,1)} %get-tuple-element.140, s32[1024]{0:T(1024)S(1)} %pad_clamp_fusion.4), kind=kCustom, calls=%fused_computation.clone.clone.1 | custom fusion | bytes 524320 | tf_op jit(solution)/shard_map/while/body/eval_jaxpr/jit(_take)/gather | solution.py:67
  136.5 3.5 %broadcast_select_fusion.4 = (bf16[8,128,4,32]{3,2,1,0:T(4,128)(2,1)}, bf16[8,128,4,32]{3,2,1,0:T(4,128)(2,1)}) fusion(bf16[8,128,4,32]{3,2,1,0:T(4,128)(2,1)S(1)} %gather_fusion, pred[8]{0:T(512)(128)(4,1)S(1)} %get-tuple-element.118, bf16[8,128,4,32]{3,2,1,0:T(4,128)(2,1)} %gather_fusion.1), kind=kLoop, calls=%fused_computation.15.clone.1 | loop fusion | flops 262144 | bytes 1048584 | tf_op jit(solution)/shard_map/while/body/eval_jaxpr/jit(_take)/select_n | solution.py:66
  140.1 3.4 %fusion.86 = (f32[4,4,128]{2,1,0:T(4,128)S(1)}, f32[4,4,128,256]{3,2,1,0:T(8,128)}) fusion(bf16[4,256,4,32]{3,2,1,0:T(4,128)(2,1)} %bitcast.73, bf16[4,4,128,4,32]{2,4,3,1,0:T(8,128)(2,1)S(1)} %get-tuple-element.141, s32[]{:T(128)} %get-tuple-element.130), kind=kOutput, calls=%fused_computation.75.clone.1 | convolution fusion | flops 35127552 | bytes 2498564 | tf_op jit(solution)/shard_map/while/body/eval_jaxpr/sub | solution.py:75
  143.4 2.3 %fusion.87 = bf16[1,4,128,4,32]{2,4,3,1,0:T(8,128)(2,1)S(1)} fusion(bf16[4,256,4,32]{3,2,1,0:T(4,128)(2,1)S(1)} %bitcast.72, f32[4,4,128,256]{3,2,1,0:T(8,128)} %get-tuple-element.121, f32[4,4,128]{2,1,0:T(4,128)S(1)} %get-tuple-element.122), kind=kOutput, calls=%fused_computation.10.clone.1 | convolution fusion | flops 34668544 | bytes 2498560 | tf_op jit(solution)/shard_map/while/body/eval_jaxpr/ghqk,gkhe->gqhe/dot_general | solution.py:77
  145.7 0.8 copy_dynamic-update-slice_fusion.2
  146.5 3.0 %gather_fusion = bf16[8,128,4,32]{3,2,1,0:T(4,128)(2,1)S(1)} fusion(bf16[16,128,4,32]{3,2,1,0:T(4,128)(2,1)} %get-tuple-element.142, s32[1024]{0:T(1024)S(1)} %pad_clamp_fusion.4), kind=kCustom, calls=%fused_computation.1.clone.clone.1 | custom fusion | bytes 524320 | tf_op jit(solution)/shard_map/while/body/eval_jaxpr/jit(_take)/gather | solution.py:66
  149.6 4.0 %gather_fusion.1 = bf16[8,128,4,32]{3,2,1,0:T(4,128)(2,1)} fusion(bf16[16,128,4,32]{3,2,1,0:T(4,128)(2,1)} %get-tuple-element.140, s32[1024]{0:T(1024)S(1)} %pad_clamp_fusion.4), kind=kCustom, calls=%fused_computation.clone.clone.1 | custom fusion | bytes 524320 | tf_op jit(solution)/shard_map/while/body/eval_jaxpr/jit(_take)/gather | solution.py:67
  153.6 3.5 %broadcast_select_fusion.4 = (bf16[8,128,4,32]{3,2,1,0:T(4,128)(2,1)}, bf16[8,128,4,32]{3,2,1,0:T(4,128)(2,1)}) fusion(bf16[8,128,4,32]{3,2,1,0:T(4,128)(2,1)S(1)} %gather_fusion, pred[8]{0:T(512)(128)(4,1)S(1)} %get-tuple-element.118, bf16[8,128,4,32]{3,2,1,0:T(4,128)(2,1)} %gather_fusion.1), kind=kLoop, calls=%fused_computation.15.clone.1 | loop fusion | flops 262144 | bytes 1048584 | tf_op jit(solution)/shard_map/while/body/eval_jaxpr/jit(_take)/select_n | solution.py:66
  157.1 3.4 %fusion.86 = (f32[4,4,128]{2,1,0:T(4,128)S(1)}, f32[4,4,128,256]{3,2,1,0:T(8,128)}) fusion(bf16[4,256,4,32]{3,2,1,0:T(4,128)(2,1)} %bitcast.73, bf16[4,4,128,4,32]{2,4,3,1,0:T(8,128)(2,1)S(1)} %get-tuple-element.141, s32[]{:T(128)} %get-tuple-element.130), kind=kOutput, calls=%fused_computation.75.clone.1 | convolution fusion | flops 35127552 | bytes 2498564 | tf_op jit(solution)/shard_map/while/body/eval_jaxpr/sub | solution.py:75
  160.5 2.3 %fusion.87 = bf16[1,4,128,4,32]{2,4,3,1,0:T(8,128)(2,1)S(1)} fusion(bf16[4,256,4,32]{3,2,1,0:T(4,128)(2,1)S(1)} %bitcast.72, f32[4,4,128,256]{3,2,1,0:T(8,128)} %get-tuple-element.121, f32[4,4,128]{2,1,0:T(4,128)S(1)} %get-tuple-element.122), kind=kOutput, calls=%fused_computation.10.clone.1 | convolution fusion | flops 34668544 | bytes 2498560 | tf_op jit(solution)/shard_map/while/body/eval_jaxpr/ghqk,gkhe->gqhe/dot_general | solution.py:77
  162.8 0.8 copy_dynamic-update-slice_fusion.2
  163.5 2.1 %all_to_all.33 = bf16[4,512,128]{1,2,0:T(8,128)(2,1)} reshape(bf16[4,4,128,4,32]{2,1,4,3,0:T(4,128)(2,1)} %get-tuple-element.38) | data formatting | bytes 1048576 | tf_op jit(solution)/shard_map/all_to_all | solution.py:83
  165.7 3.6 %all-to-all-start.2 = ((bf16[4,512,128]{1,2,0:T(8,128)(2,1)}), bf16[4,512,128]{1,2,0:T(8,128)(2,1)S(1)}, u32[]{:S(2)}, u32[]{:S(2)}) async-start(bf16[4,512,128]{1,2,0:T(8,128)(2,1)} %all_to_all.33), calls=%async_computation.2 | async-start | bytes 1048576 | tf_op jit(solution)/shard_map/all_to_all | solution.py:83
  169.3 0.0 copy-done.6
  169.3 0.0 copy-start.9
  169.3 0.2 copy.30
  169.5 6.5 %all-to-all-done.2 = bf16[4,512,128]{1,2,0:T(8,128)(2,1)S(1)} async-done(((bf16[4,512,128]{1,2,0:T(8,128)(2,1)}), bf16[4,512,128]{1,2,0:T(8,128)(2,1)S(1)}, u32[]{:S(2)}, u32[]{:S(2)}) %all-to-all-start.2) | async-done | bytes 524320 | tf_op jit(solution)/shard_map/all_to_all | solution.py:83
  176.0 2.5 %multiply_reduce_fusion.1 = (f32[512]{0:T(512)S(1)}, f32[512,512]{0,1:T(8,128)}) fusion(bf16[512,512]{0,1:T(8,128)(2,1)S(1)} %bitcast.80, bf16[512,512]{1,0:T(8,128)(2,1)} %param.20, bf16[512,512]{0,1:T(8,128)(2,1)S(1)} %copy.30), kind=kOutput, calls=%fused_computation.52 | convolution fusion | flops 269483520 | bytes 2623488 | tf_op jit(solution)/shard_map/dot_general | solution.py:84
  178.5 0.0 all-gather.5.cloned.1.call-done
  178.5 5.7 %fusion.52 = bf16[512,512]{0,1:T(8,128)(2,1)S(1)} fusion(bf16[2048,512]{1,0:T(8,128)(2,1)} %all-gather.5.cloned.1.call-done, f32[512]{0:T(512)S(1)} %copy-done.9, f32[512,512]{0,1:T(8,128)} %get-tuple-element.73, f32[512]{0:T(512)S(1)} %add_rsqrt_fusion, bf16[2048,512]{1,0:T(8,128)(2,1)} %all-gather.3.cloned.1.call-done), kind=kOutput, calls=%fused_computation.49 | convolution fusion | flops 2159280128 | bytes 5771264 | tf_op jit(solution)/shard_map/dot_general | solution.py:96
  184.2 1.0 copy.39
  (38 shorter events, 0.1 us)
Async XLA Ops:
  6.5 45.7 %copy-start = (bf16[512,1536]{1,0:T(8,128)(2,1)S(1)}, bf16[512,1536]{1,0:T(8,128)(2,1)}, u32[]{:S(2)}) copy-start(bf16[512,1536]{1,0:T(8,128)(2,1)} %param.19) | copy-start | bytes 4718596
  9.6 8.4 %copy-start.7 = (s32[4,6]{1,0:T(4,128)S(1)}, s32[4,6]{1,0:T(4,128)}, u32[]{:S(2)}) copy-start(s32[4,6]{1,0:T(4,128)} %param.16) | copy-start | bytes 292
  10.8 7.3 %copy-start.4 = (s32[4,6,128,128]{3,2,1,0:T(8,128)S(1)}, s32[4,6,128,128]{3,2,1,0:T(8,128)}, u32[]{:S(2)}) copy-start(s32[4,6,128,128]{3,2,1,0:T(8,128)} %param.15) | copy-start | bytes 4718596
  10.8 33.2 %all-to-all-start = ((bf16[8,128,512]{2,1,0:T(8,128)(2,1)}), bf16[8,128,512]{2,1,0:T(8,128)(2,1)}, u32[]{:S(2)}, u32[]{:S(2)}) async-start(bf16[8,128,512]{2,1,0:T(8,128)(2,1)} %broadcast_select_fusion.2), calls=%async_computation | async-start | bytes 2097152 | tf_op jit(solution)/shard_map/all_to_all | solution.py:32
  17.3 161.2 %all-gather.3.cloned.1.call-start = ((), (), s32[]{:S(2)}) async-start(), calls=%async_computation.3 | async-start | bytes 2621440 | tf_op jit(solution)/shard_map/all_gather | solution.py:91
  51.3 0.8 copy-start.5
  54.8 4.6 %copy-start.8 = (s32[16,2]{0,1:T(2,128)S(1)}, s32[16,2]{0,1:T(2,128)}, u32[]{:S(2)}) copy-start(s32[16,2]{0,1:T(2,128)} %param.18) | copy-start | bytes 388
  54.8 28.6 %all-to-all-start.1 = ((bf16[512,4,384]{0,2,1:T(8,128)(2,1)}), bf16[512,4,384]{0,2,1:T(8,128)(2,1)S(1)}, u32[]{:S(2)}, u32[]{:S(2)}) async-start(bf16[512,4,384]{0,2,1:T(8,128)(2,1)} %bitcast.75), calls=%async_computation.1 | async-start | bytes 3145728 | tf_op jit(solution)/shard_map/all_to_all | solution.py:51
  58.6 119.9 %all-gather.5.cloned.1.call-start = ((), (), s32[]{:S(2)}) async-start(), calls=%async_computation.4 | async-start | bytes 2621440 | tf_op jit(solution)/shard_map/all_gather | solution.py:98
  89.6 3.6 %copy-start.2 = (bf16[16,128,4,32]{1,0,3,2:T(8,128)(2,1)S(1)}, bf16[16,128,4,32]{1,0,3,2:T(8,128)(2,1)}, u32[]{:S(2)}) copy-start(bf16[16,128,4,32]{1,0,3,2:T(8,128)(2,1)} %get-tuple-element.69) | copy-start | bytes 1572868
  89.6 5.7 %copy-start.3 = (bf16[16,128,4,1,32]{1,0,4,3,2:T(8,128)(2,1)S(1)}, bf16[16,128,4,1,32]{1,0,4,3,2:T(8,128)(2,1)}, u32[]{:S(2)}) copy-start(bf16[16,128,4,1,32]{1,0,4,3,2:T(8,128)(2,1)} %get-tuple-element.70) | copy-start | bytes 1572868
  106.0 3.4 %copy-start.1 = (bf16[8,128,4,32]{3,2,1,0:T(4,128)(2,1)S(1)}, bf16[8,128,4,32]{3,2,1,0:T(4,128)(2,1)}, u32[]{:S(2)}) copy-start(bf16[8,128,4,32]{3,2,1,0:T(4,128)(2,1)} %get-tuple-element.119) | copy-start | bytes 786436 | tf_op jit(solution)/shard_map/while
  123.1 3.4 %copy-start.1 = (bf16[8,128,4,32]{3,2,1,0:T(4,128)(2,1)S(1)}, bf16[8,128,4,32]{3,2,1,0:T(4,128)(2,1)}, u32[]{:S(2)}) copy-start(bf16[8,128,4,32]{3,2,1,0:T(4,128)(2,1)} %get-tuple-element.119) | copy-start | bytes 786436 | tf_op jit(solution)/shard_map/while
  140.1 3.4 %copy-start.1 = (bf16[8,128,4,32]{3,2,1,0:T(4,128)(2,1)S(1)}, bf16[8,128,4,32]{3,2,1,0:T(4,128)(2,1)}, u32[]{:S(2)}) copy-start(bf16[8,128,4,32]{3,2,1,0:T(4,128)(2,1)} %get-tuple-element.119) | copy-start | bytes 786436 | tf_op jit(solution)/shard_map/while
  157.1 3.4 %copy-start.1 = (bf16[8,128,4,32]{3,2,1,0:T(4,128)(2,1)S(1)}, bf16[8,128,4,32]{3,2,1,0:T(4,128)(2,1)}, u32[]{:S(2)}) copy-start(bf16[8,128,4,32]{3,2,1,0:T(4,128)(2,1)} %get-tuple-element.119) | copy-start | bytes 786436 | tf_op jit(solution)/shard_map/while
  163.5 5.8 %copy-start.6 = (bf16[4,128,512]{2,1,0:T(8,128)(2,1)S(1)}, bf16[4,128,512]{2,1,0:T(8,128)(2,1)}, u32[]{:S(2)}) copy-start(bf16[4,128,512]{2,1,0:T(8,128)(2,1)} %copy-done.5) | copy-start | bytes 1572868
  165.7 10.4 %all-to-all-start.2 = ((bf16[4,512,128]{1,2,0:T(8,128)(2,1)}), bf16[4,512,128]{1,2,0:T(8,128)(2,1)S(1)}, u32[]{:S(2)}, u32[]{:S(2)}) async-start(bf16[4,512,128]{1,2,0:T(8,128)(2,1)} %all_to_all.33), calls=%async_computation.2 | async-start | bytes 1048576 | tf_op jit(solution)/shard_map/all_to_all | solution.py:83
  169.3 9.2 %copy-start.9 = (f32[512]{0:T(512)S(1)}, f32[512]{0:T(512)}, u32[]{:S(2)}) copy-start(f32[512]{0:T(512)} %param.21) | copy-start | bytes 6148
Sparse Core Ops, SparseCore 0:
  19.9 36.7 all-gather.2
  61.3 39.6 all-gather.4
where the time goes:
time: 193 us; the launch traced here: 192 us
  waiting for transfers between devices  57.4 us (30%)
  local copies, waits for them, and re-layouts  53.4 us (28%)
  matrix products  35.2 us (18%)
  other arithmetic  18.5 us (10%)
  starting transfers between devices  14 us (7%)
  between operations  13.6 us (7%)
    all_to_all x1, waiting for transfers between devices, shards(): lax.all_to_all(outgoing, 'dom', split_axis=0, concat_axis=0, tiled=True)  25.7 us
    all_to_all x1, waiting for transfers between devices, shards(): lax.all_to_all(qkv_all, 'head', split_axis=1, concat_axis=0, tiled=True)  23.9 us
    gather x4, local copies, waits for them, and re-layouts, attend(): jnp.take(values, chosen_ids, axis=0).reshape(group, -1, local_heads, HDIM)  15.9 us
    select_n x4, other arithmetic, attend(): jnp.take(keys, chosen_ids, axis=0).reshape(group, -1, local_heads, HDIM)  14.1 us
    sub x4, matrix products, attend(): exp_terms = jnp.exp(scores - row_max)  13.4 us
    gather x4, local copies, waits for them, and re-layouts, attend(): jnp.take(keys, chosen_ids, axis=0).reshape(group, -1, local_heads, HDIM)  12.1 us
    dot_general x4, matrix products, attend(): jnp.einsum('ghqk,gkhe->gqhe', attn_weights, chosen_values, preferred_elem...  9.2 us
    all_to_all x1, waiting for transfers between devices, shards(): lax.all_to_all(context, 'head', split_axis=0, concat_axis=1, tiled=True)  6.46 us
  transfers between devices with their start and end apart: 5, of which 3 were waited for; matrix products, arithmetic and copies ran while one was open for 48% of the time, Pallas kernels for 0%

commit v1 on v0

v1 whole, which is shorter than its diff:
```python
import functools
import math

import jax
import jax.numpy as jnp
from jax import lax
from jax.experimental import pallas as pl
from jax.experimental.pallas import tpu as pltpu
from jax.sharding import PartitionSpec as P

HEADS = 16
HDIM = 32
LANES = 128
CHUNKS = 2
PER_GROUP = LANES // HDIM
GROUPS = HEADS // PER_GROUP
MESH = pl.DeviceIdType.MESH
F32 = jnp.float32
BF16 = jnp.bfloat16


def dot(a, b):
    return lax.dot_general(a, b, (((1,), (0,)), ((), ())), preferred_element_type=F32)


def dot_t(a, b):
    return lax.dot_general(a, b, (((1,), (1,)), ((), ())), preferred_element_type=F32)


def kernel(
    nd,
    nh,
    features,
    pattern_hbm,
    tile_source,
    serve,
    key_blocks,
    qkv_hbm,
    attn_hbm,
    gain,
    expand_hbm,
    reduce_hbm,
    out,
    *scratch,
):
    stage = scratch[:CHUNKS]
    table = scratch[CHUNKS : 2 * CHUNKS]
    gathered = scratch[2 * CHUNKS : 3 * CHUNKS]
    (
        pattern,
        pattern16,
        scale_rows,
        qkv_raw,
        weight_q,
        weight_kv,
        weight_o,
        expand,
        reduce_w,
        queries,
        context,
        normed,
        total,
        local_sem,
        dom_send,
        dom_recv,
        agg_send,
        agg_recv,
        w_send,
        w_recv,
        fwd_send,
        fwd_recv,
    ) = scratch[3 * CHUNKS :]
    d = lax.axis_index("dom")
    h = lax.axis_index("head")
    blk, tiles, rows, _ = pattern.shape
    width = features.shape[2]
    nodes = blk * rows
    cw = width // CHUNKS
    shard = expand_hbm.shape[0]
    half = shard // 2
    core = lax.rem(d, 2)
    sibling = d + 1 - 2 * core
    dom_peers = [lax.rem(d + k, nd) for k in range(1, nd)]
    head_peers = [lax.rem(h + k, nh) for k in range(1, nh)]

    barrier = pltpu.get_barrier_semaphore()
    for p in dom_peers:
        pl.semaphore_signal(barrier, inc=1, device_id=(p, h), device_id_type=MESH)
    for q in head_peers:
        pl.semaphore_signal(barrier, inc=1, device_id=(d, q), device_id_type=MESH)

    loads = [
        pltpu.make_async_copy(pattern_hbm, pattern, local_sem.at[0]),
        pltpu.make_async_copy(qkv_hbm, qkv_raw, local_sem.at[1]),
        pltpu.make_async_copy(attn_hbm, weight_o, local_sem.at[2]),
        pltpu.make_async_copy(expand_hbm, expand.at[pl.ds(h * shard, shard)], local_sem.at[3]),
        pltpu.make_async_copy(reduce_hbm, reduce_w.at[pl.ds(h * shard, shard)], local_sem.at[4]),
    ]
    for copy in loads:
        copy.start()

    for c in range(CHUNKS):
        for p in dom_peers:
            stage[c][p] = features[serve[0, 0, p, 0], :, c * cw : (c + 1) * cw]

    def dom_copy(c, to, slot, send, recv):
        return pltpu.make_async_remote_copy(
            src_ref=stage[c].at[to],
            dst_ref=table[c].at[blk + slot],
            send_sem=dom_send.at[c, send],
            recv_sem=dom_recv.at[c, recv],
            device_id=(to, h),
            device_id_type=MESH,
        )

    def agg_copy(c, to, owner):
        part = gathered[c].at[pl.ds(owner * blk, blk)]
        return pltpu.make_async_remote_copy(
            src_ref=part,
            dst_ref=part,
            send_sem=agg_send.at[c, to],
            recv_sem=agg_recv.at[c, owner],
            device_id=(d, to),
            device_id_type=MESH,
        )

    def weight_copy(which, to, owner):
        source = (expand_hbm, reduce_hbm)[which]
        target = (expand, reduce_w)[which]
        return pltpu.make_async_remote_copy(
            src_ref=source.at[pl.ds(core * half, half)],
            dst_ref=target.at[pl.ds(owner * shard + core * half, half)],
            send_sem=w_send.at[which, to],
            recv_sem=w_recv.at[which, owner],
            device_id=(d, to),
            device_id_type=MESH,
        )

    def forward_copy(which, owner, side):
        part = (expand, reduce_w)[which].at[pl.ds(owner * shard + side * half, half)]
        return pltpu.make_async_remote_copy(
            src_ref=part,
            dst_ref=part,
            send_sem=fwd_send.at[which, owner],
            recv_sem=fwd_recv.at[which, owner],
            device_id=(sibling, h),
            device_id_type=MESH,
        )

    pl.semaphore_wait(barrier, nd + nh - 2)
    for c in range(CHUNKS):
        for p in dom_peers:
            dom_copy(c, p, d, p, d).start()
    for which in range(2):
        for q in head_peers:
            weight_copy(which, q, h).start()

    for c in range(CHUNKS):
        for b in range(blk):
            table[c][b] = features[b, :, c * cw : (c + 1) * cw]
        table[c][blk + d] = features[serve[0, 0, d, 0], :, c * cw : (c + 1) * cw]

    loads[0].wait()
    for b in range(blk):
        tile_sum = pattern[b, 0]
        for t in range(tiles):
            tile = pattern[b, t]
            pattern16[b, :, t * rows : (t + 1) * rows] = tile.astype(F32).astype(BF16)
            if t:
                tile_sum = tile_sum + tile
        degree = jnp.sum(tile_sum.astype(F32), axis=1, keepdims=True)
        scale_rows[b] = jnp.broadcast_to(lax.rsqrt(1.0 + degree), (rows, LANES))

    loads[1].wait()
    span = 3 * LANES
    source_col = lax.broadcasted_iota(jnp.int32, (span, span), 0)
    target_col = lax.broadcasted_iota(jnp.int32, (span, span), 1)
    kind = target_col // LANES
    head = (target_col // HDIM) % PER_GROUP
    entry = target_col % HDIM
    reorder = (source_col == (3 * head + kind) * HDIM + entry).astype(F32).astype(BF16)
    for g in range(GROUPS):
        moved = dot(qkv_raw[:, g * span : (g + 1) * span], reorder).astype(BF16)
        lo = g * LANES
        weight_q[:, lo : lo + LANES] = moved[:, :LANES]
        weight_kv[:, lo : lo + LANES] = moved[:, LANES : 2 * LANES]
        weight_kv[:, width + lo : width + lo + LANES] = moved[:, 2 * LANES :]
    for copy in loads[2:]:
        copy.wait()

    for c in range(CHUNKS):
        for p in dom_peers:
            dom_copy(c, d, p, d, p).wait_recv()
        for b in range(blk):
            sources = jnp.concatenate([table[c][tile_source[b, t]] for t in range(tiles)], axis=0)
            summed = dot(pattern16[b], sources)
            own = features[b, :, c * cw : (c + 1) * cw].astype(F32)
            scaled = (own + summed) * scale_rows[b, :, 0:1]
            gathered[c][h * blk + b] = scaled.astype(BF16)
        for q in head_peers:
            agg_copy(c, q, h).start()

    own_rows = jnp.concatenate(
        [gathered[c][pl.ds(h * blk, blk)].reshape(nodes, cw) for c in range(CHUNKS)], axis=1
    )
    queries[...] = dot(own_rows, weight_q[...]).astype(BF16)

    for which in range(2):
        for q in head_peers:
            weight_copy(which, h, q).wait_recv()
            forward_copy(which, q, core).start()

    for c in range(CHUNKS):
        for q in head_peers:
            agg_copy(c, h, q).wait_recv()

    chosen = key_blocks.shape[1]
    lane_head = lax.broadcasted_iota(jnp.int32, (rows, LANES), 1) // HDIM
    factor = math.log2(math.e) / math.sqrt(HDIM)

    def attend(b, carry):
        ids = [key_blocks[h * blk + b, k] for k in range(chosen)]
        picked = jnp.concatenate(
            [
                jnp.concatenate([gathered[c][i] for c in range(CHUNKS)], axis=1)
                for i in ids
            ],
            axis=0,
        )
        pairs = dot(picked, weight_kv[...]).astype(BF16)
        at = pl.multiple_of(b * rows, rows)
        for g in range(GROUPS):
            lo = g * LANES
            query = queries[pl.ds(at, rows), lo : lo + LANES]
            zero = jnp.zeros_like(query)
            stacked = jnp.concatenate(
                [jnp.where(lane_head == a, query, zero) for a in range(PER_GROUP)], axis=0
            )
            scores = dot_t(stacked, pairs[:, lo : lo + LANES])
            row_max = jnp.max(scores, axis=1, keepdims=True)
            terms = jnp.exp2((scores - row_max) * factor)
            weights = terms * (1.0 / jnp.sum(terms, axis=1, keepdims=True))
            mixed_values = dot(weights.astype(BF16), pairs[:, width + lo : width + lo + LANES])
            merged = mixed_values[:rows]
            for a in range(1, PER_GROUP):
                merged = jnp.where(lane_head == a, mixed_values[a * rows : (a + 1) * rows], merged)
            context[pl.ds(at, rows), lo : lo + LANES] = merged.astype(BF16)
        return carry

    lax.fori_loop(0, blk, attend, 0)

    own_rows = jnp.concatenate(
        [gathered[c][pl.ds(h * blk, blk)].reshape(nodes, cw) for c in range(CHUNKS)], axis=1
    )
    mixed = own_rows.astype(F32) + dot(context[...], weight_o[...])
    mean_square = jnp.mean(mixed * mixed, axis=1, keepdims=True)
    normed[...] = (mixed * lax.rsqrt(mean_square + 1e-06) * gain[...]).astype(BF16)

    for which in range(2):
        for q in head_peers:
            forward_copy(which, q, 1 - core).wait_recv()

    total[...] = normed[...].astype(F32)
    step = 512

    def feed(i, carry):
        at = pl.multiple_of(i * step, step)
        expanded = dot_t(normed[...], expand[pl.ds(at, step)])
        activated = jax.nn.gelu(expanded).astype(BF16)
        total[...] += dot(activated, reduce_w[pl.ds(at, step)])
        return carry

    lax.fori_loop(0, nh * shard // step, feed, 0)
    out[...] = total[...].astype(BF16)

    for c in range(CHUNKS):
        for p in dom_peers:
            dom_copy(c, p, d, p, d).wait_send()
        for q in head_peers:
            agg_copy(c, q, h).wait_send()
    for which in range(2):
        for q in head_peers:
            weight_copy(which, q, h).wait_send()
            forward_copy(which, q, core).wait_send()


def solution(mesh):
    nd, nh = mesh.shape["dom"], mesh.shape["head"]

    def shards(
        features,
        tile_pattern,
        tile_source,
        serve_list,
        key_blocks,
        qkv_weight,
        attn_weight,
        norm_gain,
        expand_weight,
        reduce_weight,
    ):
        blk, tiles, rows, _ = tile_pattern.shape
        nodes, width = features.shape
        cw = width // CHUNKS
        ff = expand_weight.shape[0] * nh
        vmem = pl.BlockSpec(memory_space=pltpu.VMEM)
        smem = pl.BlockSpec(memory_space=pltpu.SMEM)
        hbm = pl.BlockSpec(memory_space=pl.ANY)
        scratch = (
            [pltpu.VMEM((nd, rows, cw), BF16) for _ in range(CHUNKS)]
            + [pltpu.VMEM((blk + nd, rows, cw), BF16) for _ in range(CHUNKS)]
            + [pltpu.VMEM((nh * blk, rows, cw), BF16) for _ in range(CHUNKS)]
            + [
                pltpu.VMEM(tile_pattern.shape, jnp.int32),
                pltpu.VMEM((blk, rows, tiles * rows), BF16),
                pltpu.VMEM((blk, rows, LANES), F32),
                pltpu.VMEM(qkv_weight.shape, BF16),
                pltpu.VMEM((width, width), BF16),
                pltpu.VMEM((width, 2 * width), BF16),
                pltpu.VMEM(attn_weight.shape, BF16),
                pltpu.VMEM((ff, width), BF16),
                pltpu.VMEM((ff, width), BF16),
                pltpu.VMEM((nodes, width), BF16),
                pltpu.VMEM((nodes, width), BF16),
                pltpu.VMEM((nodes, width), BF16),
                pltpu.VMEM((nodes, width), F32),
                pltpu.SemaphoreType.DMA((5,)),
                pltpu.SemaphoreType.DMA((CHUNKS, nd)),
                pltpu.SemaphoreType.DMA((CHUNKS, nd)),
                pltpu.SemaphoreType.DMA((CHUNKS, nh)),
                pltpu.SemaphoreType.DMA((CHUNKS, nh)),
                pltpu.SemaphoreType.DMA((2, nh)),
                pltpu.SemaphoreType.DMA((2, nh)),
                pltpu.SemaphoreType.DMA((2, nh)),
                pltpu.SemaphoreType.DMA((2, nh)),
            ]
        )
        return pl.pallas_call(
            functools.partial(kernel, nd, nh),
            out_shape=jax.ShapeDtypeStruct((nodes, width), BF16),
            in_specs=[vmem, hbm, smem, smem, smem, hbm, hbm, vmem, hbm, hbm],
            out_specs=vmem,
            scratch_shapes=scratch,
            compiler_params=pltpu.CompilerParams(
                collective_id=0, has_side_effects=True, vmem_limit_bytes=56 * 1024 * 1024
            ),
        )(
            features.reshape(blk, rows, width),
            tile_pattern,
            tile_source,
            serve_list,
            key_blocks,
            qkv_weight,
            attn_weight,
            norm_gain.reshape(1, -1),
            expand_weight,
            reduce_weight,
        )

    placed = (
        P(("dom", "head"), None),
        P(("dom", "head"), None, None, None),
        P(("dom", "head"), None),
        P("dom", "head", None, None),
        P("dom", None),
        P(),
        P(),
        P(),
        P("head", None),
        P("head", None),
    )
    return jax.shard_map(
        shards, mesh=mesh, in_specs=placed, out_specs=P(("dom", "head"), None), check_vma=False
    )
```

time: 193 us -> 71.7 us (0.37)
  Pallas kernels: 0 us -> 66.9 us
  waiting for transfers between devices: 57.4 us -> 0 us
  local copies, waits for them, and re-layouts: 53.4 us -> 4.54 us
  matrix products: 35.2 us -> 0 us
  other arithmetic: 18.5 us -> 0 us
  starting transfers between devices: 14 us -> 0 us
  between operations: 13.6 us -> 0.01 us
    pallas_call x0 -> x1, Pallas kernels: none -> 66.9 us  [shards(): pl.pallas_call(functools.partial(kernel, nd, nh), out_shape=jax.ShapeDtyp...]
    all_to_all x3 -> x0, waiting for transfers between devices: 56 us -> none  [the longest x1 25.7 us: shards(): lax.all_to_all(outgoing, 'dom', split_axis=0, concat_axis=0, tiled=True)]
    gather x10 -> x0, local copies, waits for them, and re-layouts: 32.2 us -> none  [the longest x4 15.9 us: attend(): jnp.take(values, chosen_ids, axis=0).reshape(group, -1, local_heads, HDIM)]
    dot_general x8 -> x0, matrix products: 21.7 us -> none  [the longest x4 9.2 us: attend(): jnp.einsum('ghqk,gkhe->gqhe', attn_weights, chosen_values, preferred_elem...]
    select_n x7 -> x0, other arithmetic: 16.1 us -> none  [the longest x4 14.1 us: attend(): jnp.take(keys, chosen_ids, axis=0).reshape(group, -1, local_heads, HDIM)]
    all_to_all x3 -> x0, starting transfers between devices: 14 us -> none  [the longest x1 6.46 us: shards(): lax.all_to_all(outgoing, 'dom', split_axis=0, concat_axis=0, tiled=True)]
    sub x4 -> x0, matrix products: 13.4 us -> none  [attend(): exp_terms = jnp.exp(scores - row_max)]
    all_to_all x3 -> x0, local copies, waits for them, and re-layouts: 6.09 us -> none  [the longest x2 3.97 us: shards(): lax.all_to_all(qkv_all, 'head', split_axis=1, concat_axis=0, tiled=True)]
  transfers between devices with their start and end apart: 5 -> 0, of which waited for: 3 -> 0; matrix products, arithmetic and copies ran while one was open for 48% -> 0% of each run, Pallas kernels for 0% -> 0%
where the time goes in v1:
time: 71.7 us; the launch traced here: 71.5 us
  Pallas kernels  66.9 us (93%)
  local copies, waits for them, and re-layouts  4.54 us (6%)
    pallas_call x1, Pallas kernels, shards(): pl.pallas_call(functools.partial(kernel, nd, nh), out_shape=jax.ShapeDtyp...  66.9 us
    unnamed x3, local copies, waits for them, and re-layouts  4.54 us

profile of v1, /device:TPU:0, one launch (start us, length us, event | category | flops | bytes accessed | tf_op | source)
XLA Modules:
  0.0 71.5 jit_solution(4209032366172101030)
XLA Ops:
  0.0 1.3 %copy.11.serve = s32[1,1,8,1]{3,2,1,0:T(8,128)} copy(s32[1,1,8,1]{2,3,1,0:T(1,128)} %param.13) | data formatting | bytes 64 | tf_op args[3]
  1.3 1.4 %copy.12.key_blocks = s32[16,2]{1,0:T(8,128)} copy(s32[16,2]{0,1:T(2,128)} %param.14) | data formatting | bytes 256 | tf_op args[4]
  2.7 66.9 %shard_map.100 = bf16[512,512]{1,0:T(8,128)(2,1)} custom-call(bf16[4,128,512]{2,1,0:T(8,128)(2,1)} %bitcast.2, s32[4,6,128,128]{3,2,1,0:T(8,128)} %pattern_hbm.1, s32[4,6]{1,0:T(4,128)} %tile_source.1, s32[1,1,8,1]{3,2,1,0:T(8,128)} %copy.11.serve, s32[16,2]{1,0:T(8,128)} %copy.12.key_blocks, bf16[512,1536]{1,0:T(8,128)(2,1)} %qkv_hbm.1, ...), custom_call_target="tpu_custom_call" | custom-call | tf_op jit(solution)/shard_map/pallas_call | solution.py:338
  69.6 1.9 %copy.14 = bf16[512,512]{1,0:T(8,128)(2,1)} copy(bf16[512,512]{1,0:T(8,128)(2,1)} %shard_map.100) | data formatting | bytes 1048576

commit v2 on v1

--- a/solution.py
+++ b/solution.py
@@ -11,9 +11,11 @@
 HEADS = 16
 HDIM = 32
 LANES = 128
-CHUNKS = 2
+CHUNKS = 4
+DEPTH = 2
 PER_GROUP = LANES // HDIM
 GROUPS = HEADS // PER_GROUP
+FETCH_STEP = 1
 MESH = pl.DeviceIdType.MESH
 F32 = jnp.float32
 BF16 = jnp.bfloat16
@@ -67,6 +69,8 @@
         agg_recv,
         w_send,
         w_recv,
+        pair_send,
+        pair_recv,
         fwd_send,
         fwd_recv,
     ) = scratch[3 * CHUNKS :]
@@ -78,8 +82,11 @@
     cw = width // CHUNKS
     shard = expand_hbm.shape[0]
     half = shard // 2
+    quarter = shard // 4
     core = lax.rem(d, 2)
     sibling = d + 1 - 2 * core
+    pair = lax.rem(d // 2, 2)
+    partner = d + 2 - 4 * pair
     dom_peers = [lax.rem(d + k, nd) for k in range(1, nd)]
     head_peers = [lax.rem(h + k, nh) for k in range(1, nh)]
 
@@ -128,11 +135,23 @@
         source = (expand_hbm, reduce_hbm)[which]
         target = (expand, reduce_w)[which]
         return pltpu.make_async_remote_copy(
-            src_ref=source.at[pl.ds(core * half, half)],
-            dst_ref=target.at[pl.ds(owner * shard + core * half, half)],
+            src_ref=source.at[pl.ds(core * half + pair * quarter, quarter)],
+            dst_ref=target.at[pl.ds(owner * shard + core * half + pair * quarter, quarter)],
             send_sem=w_send.at[which, to],
             recv_sem=w_recv.at[which, owner],
             device_id=(d, to),
+            device_id_type=MESH,
+        )
+
+    def pair_copy(which, owner, side):
+        at = owner * shard + core * half + side * quarter
+        part = (expand, reduce_w)[which].at[pl.ds(at, quarter)]
+        return pltpu.make_async_remote_copy(
+            src_ref=part,
+            dst_ref=part,
+            send_sem=pair_send.at[which, owner],
+            recv_sem=pair_recv.at[which, owner],
+            device_id=(partner, h),
             device_id_type=MESH,
         )
 
@@ -148,7 +167,7 @@
         )
 
     pl.semaphore_wait(barrier, nd + nh - 2)
-    for c in range(CHUNKS):
+    for c in range(DEPTH):
         for p in dom_peers:
             dom_copy(c, p, d, p, d).start()
     for which in range(2):
@@ -191,6 +210,9 @@
     for c in range(CHUNKS):
         for p in dom_peers:
             dom_copy(c, d, p, d, p).wait_recv()
+        if c + DEPTH < CHUNKS:
+            for p in dom_peers:
+                dom_copy(c + DEPTH, p, d, p, d).start()
         for b in range(blk):
             sources = jnp.concatenate([table[c][tile_source[b, t]] for t in range(tiles)], axis=0)
             summed = dot(pattern16[b], sources)
@@ -199,20 +221,25 @@
             gathered[c][h * blk + b] = scaled.astype(BF16)
         for q in head_peers:
             agg_copy(c, q, h).start()
+        if c == FETCH_STEP:
+            for which in range(2):
+                for q in head_peers:
+                    weight_copy(which, h, q).wait_recv()
+                    pair_copy(which, q, pair).start()
 
     own_rows = jnp.concatenate(
         [gathered[c][pl.ds(h * blk, blk)].reshape(nodes, cw) for c in range(CHUNKS)], axis=1
     )
     queries[...] = dot(own_rows, weight_q[...]).astype(BF16)
 
+    for c in range(CHUNKS):
+        for q in head_peers:
+            agg_copy(c, h, q).wait_recv()
+
     for which in range(2):
         for q in head_peers:
-            weight_copy(which, h, q).wait_recv()
+            pair_copy(which, q, 1 - pair).wait_recv()
             forward_copy(which, q, core).start()
-
-    for c in range(CHUNKS):
-        for q in head_peers:
-            agg_copy(c, h, q).wait_recv()
 
     chosen = key_blocks.shape[1]
     lane_head = lax.broadcasted_iota(jnp.int32, (rows, LANES), 1) // HDIM
@@ -247,7 +274,8 @@
             context[pl.ds(at, rows), lo : lo + LANES] = merged.astype(BF16)
         return carry
 
-    lax.fori_loop(0, blk, attend, 0)
+    lax.fori_loop(0, blk, attend, 0, unroll=True)
+
 
     own_rows = jnp.concatenate(
         [gathered[c][pl.ds(h * blk, blk)].reshape(nodes, cw) for c in range(CHUNKS)], axis=1
@@ -270,7 +298,7 @@
         total[...] += dot(activated, reduce_w[pl.ds(at, step)])
         return carry
 
-    lax.fori_loop(0, nh * shard // step, feed, 0)
+    lax.fori_loop(0, nh * shard // step, feed, 0, unroll=True)
     out[...] = total[...].astype(BF16)
 
     for c in range(CHUNKS):
@@ -281,6 +309,7 @@
     for which in range(2):
         for q in head_peers:
             weight_copy(which, q, h).wait_send()
+            pair_copy(which, q, pair).wait_send()
             forward_copy(which, q, core).wait_send()
 
 
@@ -333,6 +362,8 @@
                 pltpu.SemaphoreType.DMA((2, nh)),
                 pltpu.SemaphoreType.DMA((2, nh)),
                 pltpu.SemaphoreType.DMA((2, nh)),
+                pltpu.SemaphoreType.DMA((2, nh)),
+                pltpu.SemaphoreType.DMA((2, nh)),
             ]
         )
         return pl.pallas_call(

time: 71.7 us -> 60.2 us (0.84)
  Pallas kernels: 66.9 us -> 55.4 us
    pallas_call x1, Pallas kernels: 66.9 us -> 55.4 us  [shards(): pl.pallas_call(functools.partial(kernel, nd, nh), out_shape=jax.ShapeDtyp...]
where the time goes in v2:
time: 60.2 us; the launch traced here: 60 us
  Pallas kernels  55.4 us (92%)
  local copies, waits for them, and re-layouts  4.54 us (8%)
    pallas_call x1, Pallas kernels, shards(): pl.pallas_call(functools.partial(kernel, nd, nh), out_shape=jax.ShapeDtyp...  55.4 us
    unnamed x3, local copies, waits for them, and re-layouts  4.54 us

profile of v2, /device:TPU:0, one launch (start us, length us, event | category | flops | bytes accessed | tf_op | source)
XLA Modules:
  0.0 60.0 jit_solution(12166338829889071892)
XLA Ops:
  0.0 1.3 %copy.11.serve = s32[1,1,8,1]{3,2,1,0:T(8,128)} copy(s32[1,1,8,1]{2,3,1,0:T(1,128)} %param.13) | data formatting | bytes 64 | tf_op args[3]
  1.3 1.4 %copy.12.key_blocks = s32[16,2]{1,0:T(8,128)} copy(s32[16,2]{0,1:T(2,128)} %param.14) | data formatting | bytes 256 | tf_op args[4]
  2.7 55.4 %shard_map.100 = bf16[512,512]{1,0:T(8,128)(2,1)} custom-call(bf16[4,128,512]{2,1,0:T(8,128)(2,1)} %bitcast.2, s32[4,6,128,128]{3,2,1,0:T(8,128)} %pattern_hbm.1, s32[4,6]{1,0:T(4,128)} %tile_source.1, s32[1,1,8,1]{3,2,1,0:T(8,128)} %copy.11.serve, s32[16,2]{1,0:T(8,128)} %copy.12.key_blocks, bf16[512,1536]{1,0:T(8,128)(2,1)} %qkv_hbm.1, ...), custom_call_target="tpu_custom_call" | custom-call | tf_op jit(solution)/shard_map/pallas_call | solution.py:369
  58.1 1.9 %copy.14 = bf16[512,512]{1,0:T(8,128)(2,1)} copy(bf16[512,512]{1,0:T(8,128)(2,1)} %shard_map.100) | data formatting | bytes 1048576

commit v3 on v2

--- a/solution.py
+++ b/solution.py
@@ -236,11 +236,6 @@
         for q in head_peers:
             agg_copy(c, h, q).wait_recv()
 
-    for which in range(2):
-        for q in head_peers:
-            pair_copy(which, q, 1 - pair).wait_recv()
-            forward_copy(which, q, core).start()
-
     chosen = key_blocks.shape[1]
     lane_head = lax.broadcasted_iota(jnp.int32, (rows, LANES), 1) // HDIM
     factor = math.log2(math.e) / math.sqrt(HDIM)
@@ -274,7 +269,15 @@
             context[pl.ds(at, rows), lo : lo + LANES] = merged.astype(BF16)
         return carry
 
-    lax.fori_loop(0, blk, attend, 0, unroll=True)
+    early = blk // 2
+    lax.fori_loop(0, early, attend, 0, unroll=True)
+
+    for which in range(2):
+        for q in head_peers:
+            pair_copy(which, q, 1 - pair).wait_recv()
+            forward_copy(which, q, core).start()
+
+    lax.fori_loop(early, blk, attend, 0, unroll=True)
 
 
     own_rows = jnp.concatenate(
@@ -284,21 +287,15 @@
     mean_square = jnp.mean(mixed * mixed, axis=1, keepdims=True)
     normed[...] = (mixed * lax.rsqrt(mean_square + 1e-06) * gain[...]).astype(BF16)
 
-    for which in range(2):
-        for q in head_peers:
-            forward_copy(which, q, 1 - core).wait_recv()
-
     total[...] = normed[...].astype(F32)
-    step = 512
-
-    def feed(i, carry):
-        at = pl.multiple_of(i * step, step)
-        expanded = dot_t(normed[...], expand[pl.ds(at, step)])
+    for q in [h] + head_peers:
+        if q is not h:
+            for which in range(2):
+                forward_copy(which, q, 1 - core).wait_recv()
+        at = pl.multiple_of(q * shard, shard)
+        expanded = dot_t(normed[...], expand[pl.ds(at, shard)])
         activated = jax.nn.gelu(expanded).astype(BF16)
-        total[...] += dot(activated, reduce_w[pl.ds(at, step)])
-        return carry
-
-    lax.fori_loop(0, nh * shard // step, feed, 0, unroll=True)
+        total[...] += dot(activated, reduce_w[pl.ds(at, shard)])
     out[...] = total[...].astype(BF16)
 
     for c in range(CHUNKS):

time: 60.2 us -> 58.8 us (0.977)
  Pallas kernels: 55.4 us -> 54.1 us
    pallas_call x1, Pallas kernels: 55.4 us -> 54.1 us  [shards(): pl.pallas_call(functools.partial(kernel, nd, nh), out_shape=jax.ShapeDtyp...]
where the time goes in v3:
time: 58.8 us; the launch traced here: 58.6 us
  Pallas kernels  54.1 us (92%)
  local copies, waits for them, and re-layouts  4.54 us (8%)
    pallas_call x1, Pallas kernels, shards(): pl.pallas_call(functools.partial(kernel, nd, nh), out_shape=jax.ShapeDtyp...  54.1 us
    unnamed x3, local copies, waits for them, and re-layouts  4.54 us

profile of v3, /device:TPU:0, one launch (start us, length us, event | category | flops | bytes accessed | tf_op | source)
XLA Modules:
  0.0 58.6 jit_solution(11285370803071105828)
XLA Ops:
  0.0 1.3 %copy.11.serve = s32[1,1,8,1]{3,2,1,0:T(8,128)} copy(s32[1,1,8,1]{2,3,1,0:T(1,128)} %param.13) | data formatting | bytes 64 | tf_op args[3]
  1.3 1.4 %copy.12.key_blocks = s32[16,2]{1,0:T(8,128)} copy(s32[16,2]{0,1:T(2,128)} %param.14) | data formatting | bytes 256 | tf_op args[4]
  2.7 54.1 %shard_map.100 = bf16[512,512]{1,0:T(8,128)(2,1)} custom-call(bf16[4,128,512]{2,1,0:T(8,128)(2,1)} %bitcast.2, s32[4,6,128,128]{3,2,1,0:T(8,128)} %pattern_hbm.1, s32[4,6]{1,0:T(4,128)} %tile_source.1, s32[1,1,8,1]{3,2,1,0:T(8,128)} %copy.11.serve, s32[16,2]{1,0:T(8,128)} %copy.12.key_blocks, bf16[512,1536]{1,0:T(8,128)(2,1)} %qkv_hbm.1, ...), custom_call_target="tpu_custom_call" | custom-call | tf_op jit(solution)/shard_map/pallas_call | solution.py:366
  56.8 1.9 %copy.14 = bf16[512,512]{1,0:T(8,128)(2,1)} copy(bf16[512,512]{1,0:T(8,128)(2,1)} %shard_map.100) | data formatting | bytes 1048576
